TPU v7x, 32 devices: a whole 2x2x4 slice. The times are simulated.
32 devices in a mesh: blk: 32 (over z, y, x, core).
Axes of the slice: x: 2, y: 2, z: 4, core: 2. Of those that a mesh axis runs over, the one named last changes fastest.
Arguments:
- positive_row: float32 [256, 8192], P(None, 'blk'), may hold values from -6 to 160, as said below
- negative_row: float32 [256, 8192], P(None, 'blk'), may hold values from -5 to 5
Outputs:
- positive_out: float32 [256, 8192], P(None, 'blk')
- negative_out: float32 [256, 8192], P(None, 'blk')
Inputs may be any that keep to these rules, and one draw needn't show every extreme that they name: `positive_row`: the first 256 columns form an upper triangular block whose diagonal lies between 80 and 160.
All inputs are finite; a program needn't handle non-finite values.
Results may differ from a plain program's by a relative error of at most 0.00017.
Values sent between devices are 32-bit elements; how exact they have to be, the bound alone decides.
A program may use at most 64 MiB of HBM per device.

v0:
```python
import jax
import jax.numpy as jnp
from jax import lax
from jax.sharding import PartitionSpec as P

STEPS = 2
NEWTON = 4


HIGHEST = lax.Precision.HIGHEST


def broadcast(array, axis, root):
    mine = lax.axis_index(axis) == root
    return lax.psum(jnp.where(mine, array, jnp.zeros_like(array)), axis)


def shifted(block, axis, distance):
    devices = range(lax.axis_size(axis))
    route = [(i - distance, i) for i in devices if i - distance in devices]
    return lax.ppermute(block, axis, route)


def identity_of(size):
    rows_index = lax.broadcasted_iota(jnp.int32, (size, size), 0)
    cols_index = lax.broadcasted_iota(jnp.int32, (size, size), 1)
    return jnp.where(rows_index == cols_index, 1.0, 0.0).astype(jnp.float32)


def root_series(gram_part, identity):
    inner = 0.3125 * identity + 0.2734375 * gram_part
    inner = 0.375 * identity + jnp.dot(gram_part, inner, precision=HIGHEST)
    inner = 0.5 * identity + jnp.dot(gram_part, inner, precision=HIGHEST)
    return identity + jnp.dot(gram_part, inner, precision=HIGHEST)


def solve_coupling(lead_p, lead_n):
    identity = identity_of(lead_p.shape[0])
    diag_values = jnp.sum(lead_p * identity, axis=1)
    approx = identity * (1.0 / diag_values)[:, None]
    lead_t = lead_p.T
    for newton_index in range(NEWTON):
        product = jnp.dot(lead_t, approx, precision=HIGHEST)
        approx = jnp.dot(approx, 2.0 * identity - product, precision=HIGHEST)
    return jnp.dot(approx, lead_n.T, precision=HIGHEST)


def empty_coupling(lead_p, lead_n):
    return jnp.zeros_like(lead_p)


def roots_from(coupling_t):
    identity = identity_of(coupling_t.shape[0])
    gram_top = jnp.dot(coupling_t, coupling_t.T, precision=HIGHEST)
    gram_bottom = jnp.dot(coupling_t.T, coupling_t, precision=HIGHEST)
    return (root_series(gram_top, identity), root_series(gram_bottom, identity))


def apply_reflector(coupling_t, root_top, root_bottom, positive, negative):
    wide_p = positive - jnp.dot(coupling_t, negative, precision=HIGHEST)
    wide_n = negative - jnp.dot(coupling_t.T, positive, precision=HIGHEST)
    new_p = jnp.dot(root_top, wide_p, precision=HIGHEST)
    new_n = jnp.dot(root_bottom, wide_n, precision=HIGHEST)
    return (new_p, new_n)


def on_device(positive_row, negative_row):
    my_index = lax.axis_index("blk")
    positive = positive_row
    negative = negative_row
    for step_index in range(STEPS):
        is_owner = my_index == step_index
        coupling_t = lax.cond(is_owner, solve_coupling, empty_coupling, positive, negative)
        coupling_t = broadcast(coupling_t, "blk", step_index)
        root_top, root_bottom = roots_from(coupling_t)
        new_p, new_n = apply_reflector(coupling_t, root_top, root_bottom, positive, negative)
        positive = shifted(new_p, "blk", 1)
        negative = new_n
    return (positive, negative)


def solution(mesh):
    in_specs = (P(None, "blk"), P(None, "blk"))
    out_specs = (P(None, "blk"), P(None, "blk"))
    return jax.shard_map(
        on_device, mesh=mesh, in_specs=in_specs, out_specs=out_specs, check_vma=False
    )
```

profile of v0, /device:TPU:16, one launch (start us, length us, event | category | flops | bytes accessed | tf_op | source)
XLA Modules:
  0.0 301.2 jit_solution(2826282831965728609)
XLA Ops:
  7.2 0.0 all-reduce.3.cloned.1.call-start
  7.3 0.7 broadcast_select_fusion.1
  8.0 0.0 all-reduce.3.cloned.1.call-update
  8.0 0.0 all-reduce.5.cloned.1.call-start
  8.1 131.0 %all-reduce.3.cloned.1.call-done = f32[256,256]{1,0:T(8,128)} async-done(((f32[256,256]{1,0:T(8,128)}), f32[256,256]{1,0:T(8,128)}) %all-reduce.3.cloned.1.call-update) | async-done | bytes 262160 | tf_op jit(solution)/shard_map/psum | solution.py:15
  139.1 1.4 fusion.84
  140.6 0.4 convolution_add_fusion.11
  141.0 0.4 convolution_add_fusion.10
  141.4 0.0 copy-start.2
  141.4 0.4 convolution_add_fusion.9
  141.8 0.6 copy-done.2
  142.3 0.6 fusion.86
  142.9 0.4 convolution_add_fusion.8
  143.3 0.0 copy-start
  143.3 0.0 copy-start.4
  143.4 0.4 convolution_add_fusion.7
  143.7 0.5 copy-done
  144.3 0.1 copy-done.4
  144.4 0.4 convolution_subtract_fusion.3
  144.7 0.4 fusion.85
  145.1 1.9 collective-permute-start
  147.1 0.6 convolution_subtract_fusion.2
  147.7 0.4 convolution_add_fusion.6
  148.1 0.4 fusion.87
  148.4 6.2 %collective-permute-done = f32[256,256]{1,0:T(8,128)S(1)} collective-permute-done((f32[256,256]{1,0:T(8,128)S(1)}, f32[256,256]{1,0:T(8,128)S(1)}, u32[]{:S(2)}, u32[]{:S(2)}) %collective-permute-start) | collective-permute-done | bytes 262176 | tf_op jit(solution)/shard_map/ppermute | solution.py:21
  154.6 0.2 conditional.3
  154.8 0.7 broadcast_select_fusion
  155.6 0.0 all-reduce.5.cloned.1.call-update
  155.6 123.2 %all-reduce.5.cloned.1.call-done = f32[256,256]{1,0:T(8,128)} async-done(((f32[256,256]{1,0:T(8,128)}), f32[256,256]{1,0:T(8,128)}) %all-reduce.5.cloned.1.call-update) | async-done | bytes 262160 | tf_op jit(solution)/shard_map/psum | solution.py:15
  278.8 1.4 fusion.88
  280.2 0.4 convolution_add_fusion.5
  280.7 0.4 convolution_add_fusion.4
  281.0 0.0 copy-start.3
  281.1 0.4 convolution_add_fusion.3
  281.4 0.6 copy-done.3
  282.0 0.6 fusion.90
  282.6 0.4 convolution_add_fusion.2
  283.0 0.4 convolution_add_fusion.1
  283.4 0.4 convolution_subtract_fusion.1
  283.8 0.4 fusion.89
  284.2 1.9 collective-permute-start.1
  286.1 0.6 convolution_subtract_fusion
  286.7 0.4 convolution_add_fusion
  287.1 1.1 fusion.91
  288.2 5.5 %collective-permute-done.1 = f32[256,256]{1,0:T(8,128)S(1)} collective-permute-done((f32[256,256]{1,0:T(8,128)S(1)}, f32[256,256]{1,0:T(8,128)S(1)}, u32[]{:S(2)}, u32[]{:S(2)}) %collective-permute-start.1) | collective-permute-done | bytes 262176 | tf_op jit(solution)/shard_map/ppermute | solution.py:21
  293.7 0.7 copy.11
  (3 shorter events, 0.1 us)
Async XLA Ops:
  7.2 131.9 %all-reduce.3.cloned.1.call-start = ((), (), s32[]{:S(2)}) async-start(), calls=%async_computation | async-start | bytes 524288 | tf_op jit(solution)/shard_map/psum | solution.py:15
  8.0 270.8 %all-reduce.5.cloned.1.call-start = ((), (), s32[]{:S(2)}) async-start(), calls=%async_computation.1 | async-start | bytes 524288 | tf_op jit(solution)/shard_map/psum | solution.py:15
  141.4 1.0 copy-start.2
  143.3 1.0 copy-start
  143.3 1.0 copy-start.4
  145.1 9.5 %collective-permute-start = (f32[256,256]{1,0:T(8,128)S(1)}, f32[256,256]{1,0:T(8,128)S(1)}, u32[]{:S(2)}, u32[]{:S(2)}) collective-permute-start(f32[256,256]{1,0:T(8,128)S(1)} %fusion.85), channel_id=1, source_target_pairs={{0,1},{1,2},{2,3},{3,4},{4,5},{5,6},{6,7},{7,8},{8,9},{9,10},{10,1... | collective-permute-start | bytes 786440 | tf_op jit(solution)/shard_map/ppermute | solution.py:21
  281.0 1.0 copy-start.3
  284.2 9.5 %collective-permute-start.1 = (f32[256,256]{1,0:T(8,128)S(1)}, f32[256,256]{1,0:T(8,128)S(1)}, u32[]{:S(2)}, u32[]{:S(2)}) collective-permute-start(f32[256,256]{1,0:T(8,128)S(1)} %fusion.89), channel_id=1, source_target_pairs={{0,1},{1,2},{2,3},{3,4},{4,5},{5,6},{6,7},{7,8},{8,9},{9,10},{10,1... | collective-permute-start | bytes 786440 | tf_op jit(solution)/shard_map/ppermute | solution.py:21
Sparse Core Ops, SparseCore 0:
  14.1 124.9 all-reduce.2
  155.7 123.0 all-reduce.4
where the time goes:
time: 303 us; the launch traced here: 301 us
  waiting for transfers between devices  266 us (88%)
  between operations  14.3 us (5%)
  matrix products  12.9 us (4%)
  starting transfers between devices  3.92 us (1%)
    psum x2, waiting for transfers between devices, broadcast(): return lax.psum(jnp.where(mine, array, jnp.zeros_like(array)), axis)  254 us
    ppermute x2, waiting for transfers between devices, shifted(): return lax.ppermute(block, axis, route)  11.7 us
  transfers between devices with their start and end apart: 4, of which 4 were waited for; matrix products, arithmetic and copies ran while one was open for 1% of the time, Pallas kernels for 0%

commit v1 on v0

v1 whole, which is shorter than its diff:
```python
import functools

import jax
import jax.numpy as jnp
from jax import lax
from jax.experimental import pallas as pl
from jax.experimental.pallas import tpu as pltpu
from jax.sharding import PartitionSpec as P

STEPS = 2
NEWTON = 4
CHUNKS = 4
MESH = pl.DeviceIdType.MESH


def tree_shape(devices):
    chips = devices // 2
    outer = 4 if chips % 4 == 0 else 1
    rest = chips // outer
    middle = 1
    while middle * middle < rest:
        middle *= 2
    return outer, middle, rest // middle


def split(a):
    high = a.astype(jnp.bfloat16)
    low = (a - high.astype(jnp.float32)).astype(jnp.bfloat16)
    return high, low


def mm(a, b):
    dot = functools.partial(jnp.dot, preferred_element_type=jnp.float32)
    return dot(a[0], b[0]) + (dot(a[0], b[1]) + dot(a[1], b[0]))


def eye_mask(size):
    rows = lax.broadcasted_iota(jnp.int32, (size, size), 0)
    cols = lax.broadcasted_iota(jnp.int32, (size, size), 1)
    return rows == cols


def solve(lead_p, lead_n):
    mask = eye_mask(lead_p.shape[0])
    diagonal = jnp.where(mask, lead_p, 0.0)
    inv_rows = 1.0 / jnp.sum(diagonal, axis=1, keepdims=True)
    inv_cols = 1.0 / jnp.sum(diagonal, axis=0, keepdims=True)
    power = jnp.where(mask, 1.0, 0.0) - inv_rows * lead_p
    acc = lead_n
    for index in range(NEWTON):
        power_s = split(power)
        acc = acc + mm(split(acc), power_s)
        if index < NEWTON - 1:
            power = mm(power_s, power_s)
    return acc * inv_cols


def root_less_one(gram):
    mask = eye_mask(gram.shape[0])
    gram_s = split(gram)
    square = mm(gram_s, gram_s)
    inner = jnp.where(mask, 0.375, 0.0) + 0.3125 * gram + 0.2734375 * square
    return 0.5 * gram + mm(split(square), split(inner))


def roots_from(kt):
    c_s = split(kt.T)
    k_s = split(kt)
    s_top = root_less_one(mm(c_s, k_s))
    s_bottom = root_less_one(mm(k_s, c_s))
    return c_s, k_s, split(s_top), split(s_bottom)


def reflect(c_s, s_s, main, other):
    wide = main - mm(c_s, split(other))
    return wide + mm(s_s, split(wide))


def kernel(n, pos_ref, neg_ref, pos_out, neg_out, lead, nb, kbuf, pair, own1,
           bc_send, bc_recv, nb_send, nb_recv, rel_send, ld_send, ld_recv):
    me = lax.axis_index("blk")
    outer, middle, inner = tree_shape(n)
    size = pos_ref.shape[0]
    rows = size // CHUNKS
    core = me % 2
    c = (me // 2) % inner
    b = (me // (2 * inner)) % middle
    a = me // (2 * inner * middle)
    y_step, z_step = 2 * inner, 2 * inner * middle
    even = core == 0
    y_child = even & (c == 0) & (b + 1 < middle)
    y_parent = even & (c == 0) & (b > 0)
    z_child = even & (c == 0) & (b == 0) & (a + 1 < outer)
    z_parent = even & (c == 0) & (b == 0) & (a > 0)
    links = [
        (me >= 1, me - 1), (me + 1 < n, me + 1), (me >= 2, me - 2), (me + 2 < n, me + 2),
        (y_child, me + y_step), (y_parent, me - y_step),
        (z_child, me + z_step), (z_parent, me - z_step),
    ]
    children = [
        (z_child, me + z_step),
        (y_child, me + y_step),
        (even & (c + 1 < inner), me + 2),
        (even & (me > 0), me + 1),
    ]

    barrier = pltpu.get_barrier_semaphore()
    count = jnp.int32(0)
    for there, device in links:
        count = count + jnp.where(there, 1, 0)

        @pl.when(there)
        def _(device=device):
            pl.semaphore_signal(barrier, inc=1, device_id=(device,), device_id_type=MESH)

    pl.semaphore_wait(barrier, count)

    def remote(src, dst, send, recv, device):
        return pltpu.make_async_remote_copy(
            src_ref=src, dst_ref=dst, send_sem=send, recv_sem=recv,
            device_id=(device,), device_id_type=MESH)

    has_next = me + 1 < n
    to_second = even & (me + 2 < n)
    next_copies = [remote(ref, nb.at[i], nb_send.at[i], nb_recv.at[i], me + 1)
                   for i, ref in enumerate((pos_ref, neg_ref))]
    second_copies = [remote(ref, nb.at[2 + i], nb_send.at[2 + i], nb_recv.at[2 + i], me + 2)
                     for i, ref in enumerate((pos_ref, neg_ref))]
    relay_copies = [remote(nb.at[i], nb.at[2 + i], rel_send.at[i], nb_recv.at[2 + i], me + 1)
                    for i in range(2)]
    lead_copies = [remote(ref, lead.at[2 + i], ld_send.at[i], ld_recv.at[i], 0)
                   for i, ref in enumerate((pos_ref, neg_ref))]

    def start(copies):
        for copy in copies:
            copy.start()

    @pl.when(has_next)
    def _():
        start(next_copies)

    @pl.when(me == 1)
    def _():
        start(lead_copies)

    @pl.when(to_second)
    def _():
        start(second_copies)

    def chunk_copy(step, chunk, child, device):
        part = kbuf.at[step, pl.ds(chunk * rows, rows)]
        return remote(part, part, bc_send.at[step, chunk, child], bc_recv.at[step, chunk], device)

    def forward(step, chunk):
        for child, (there, device) in enumerate(children):
            @pl.when(there)
            def _(child=child, device=device):
                chunk_copy(step, chunk, child, device).start()

    def receive(step):
        for chunk in range(CHUNKS):
            chunk_copy(step, chunk, 0, me).wait_recv()
            forward(step, chunk)

    def neighbours():
        @pl.when(me >= 1)
        def _():
            for copy in next_copies:
                copy.wait_recv()

    @pl.when(me < 2)
    def _():
        @pl.when(me == 0)
        def _():
            nb[...] = jnp.zeros_like(nb)
            lead[0] = pos_ref[...]
            lead[1] = neg_ref[...]
            for copy in lead_copies:
                copy.wait_recv()

        @pl.when(me == 1)
        def _():
            for copy in next_copies:
                copy.wait_recv()
            nb[2] = jnp.zeros((size, size), jnp.float32)
            nb[3] = jnp.zeros((size, size), jnp.float32)
            lead[0] = nb[0]
            lead[1] = nb[1]
            lead[2] = pos_ref[...]
            lead[3] = neg_ref[...]

        kbuf[0] = solve(lead[0], lead[1])

        @pl.when(me == 0)
        def _():
            for chunk in range(CHUNKS):
                forward(0, chunk)

    @pl.when(me >= 2)
    def _():
        receive(0)
        for copy in next_copies:
            copy.wait_recv()

        @pl.when(even)
        def _():
            start(relay_copies)

    c_s, k_s, st_s, sb_s = roots_from(kbuf[0])
    for i, pair_part in enumerate((c_s, k_s, st_s, sb_s)):
        pair[i, 0] = pair_part[0]
        pair[i, 1] = pair_part[1]

    def loaded():
        return [(pair[i, 0], pair[i, 1]) for i in range(4)]

    @pl.when(me < 2)
    def _():
        c1, k1, st1, sb1 = loaded()
        lead_p = reflect(c1, st1, lead[0], lead[1])
        lead_n = reflect(k1, sb1, lead[3], lead[2])
        kbuf[1] = solve(lead_p, lead_n)

        @pl.when(me == 0)
        def _():
            for chunk in range(CHUNKS):
                forward(1, chunk)

    @pl.when(me >= 2)
    def _():
        for copy in second_copies:
            copy.wait_recv()

    c1, k1, st1, sb1 = loaded()
    own1[0] = reflect(k1, sb1, neg_ref[...], pos_ref[...])
    own1[1] = reflect(c1, st1, nb[0], nb[1])
    own1[2] = reflect(k1, sb1, nb[1], nb[0])
    own1[3] = reflect(c1, st1, nb[2], nb[3])

    @pl.when(me >= 2)
    def _():
        receive(1)

    c2, k2, st2, sb2 = roots_from(kbuf[1])
    neg_out[...] = reflect(k2, sb2, own1[0], own1[1])
    pos_out[...] = reflect(c2, st2, own1[3], own1[2])

    @pl.when(has_next)
    def _():
        for copy in next_copies:
            copy.wait_send()

    @pl.when(me == 1)
    def _():
        for copy in lead_copies:
            copy.wait_send()

    @pl.when(to_second)
    def _():
        for copy in second_copies:
            copy.wait_send()

    @pl.when(even & (me >= 2))
    def _():
        for copy in relay_copies:
            copy.wait_send()

    for child, (there, device) in enumerate(children):
        @pl.when(there)
        def _(child=child, device=device):
            for step in range(STEPS):
                for chunk in range(CHUNKS):
                    chunk_copy(step, chunk, child, device).wait_send()


def solution(mesh):
    n = mesh.shape["blk"]

    def on_device(positive_row, negative_row):
        size = positive_row.shape[0]
        block = jax.ShapeDtypeStruct((size, size), jnp.float32)
        dma = pltpu.SemaphoreType.DMA
        vmem = pl.BlockSpec(memory_space=pltpu.VMEM)
        return pl.pallas_call(
            functools.partial(kernel, n),
            out_shape=(block, block),
            in_specs=[vmem, vmem],
            out_specs=(vmem, vmem),
            scratch_shapes=[
                pltpu.VMEM((4, size, size), jnp.float32),
                pltpu.VMEM((4, size, size), jnp.float32),
                pltpu.VMEM((STEPS, size, size), jnp.float32),
                pltpu.VMEM((4, 2, size, size), jnp.bfloat16),
                pltpu.VMEM((4, size, size), jnp.float32),
                dma((STEPS, CHUNKS, 4)), dma((STEPS, CHUNKS)),
                dma((4,)), dma((4,)), dma((2,)), dma((2,)), dma((2,)),
            ],
            compiler_params=pltpu.CompilerParams(
                collective_id=0, has_side_effects=True, vmem_limit_bytes=48 * 2**20),
        )(positive_row, negative_row)

    spec = (P(None, "blk"), P(None, "blk"))
    return jax.shard_map(on_device, mesh=mesh, in_specs=spec, out_specs=spec, check_vma=False)
```

time: 303 us -> 39.4 us (0.13)
  the two profiles are of different devices: /device:TPU:16 before, /device:TPU:31 now
where the time goes in v1:
time: 39.4 us; the launch traced here: 39.3 us
  Pallas kernels  35.3 us (90%)
  local copies, waits for them, and re-layouts  3.3 us (8%)
  between operations  0.65 us (2%)
    pallas_call x1, Pallas kernels, on_device(): pl.pallas_call(functools.partial(kernel, n), out_shape=(block, block), in...  35.3 us
    unnamed x6, local copies, waits for them, and re-layouts  3.3 us

profile of v1, /device:TPU:31, one launch (start us, length us, event | category | flops | bytes accessed | tf_op | source)
XLA Modules:
  0.0 39.3 jit_solution(14722606222267749802)
XLA Ops:
  0.6 0.0 copy-start
  0.6 0.9 %copy-done = f32[256,256]{1,0:T(8,128)S(1)} copy-done((f32[256,256]{1,0:T(8,128)S(1)}, f32[256,256]{1,0:T(8,128)}, u32[]{:S(2)}) %copy-start) | copy-done | bytes 262168
  1.6 0.0 copy-start.1
  1.6 0.9 %copy-done.1 = f32[256,256]{1,0:T(8,128)S(1)} copy-done((f32[256,256]{1,0:T(8,128)S(1)}, f32[256,256]{1,0:T(8,128)}, u32[]{:S(2)}) %copy-start.1) | copy-done | bytes 262168
  2.5 35.3 %shard_map.41 = (f32[256,256]{1,0:T(8,128)S(1)}, f32[256,256]{1,0:T(8,128)S(1)}) custom-call(f32[256,256]{1,0:T(8,128)S(1)} %copy-done, f32[256,256]{1,0:T(8,128)S(1)} %copy-done.1), custom_call_target="tpu_custom_call" | custom-call | tf_op jit(solution)/shard_map/pallas_call | solution.py:284
  37.8 0.7 %copy.6 = f32[256,256]{1,0:T(8,128)} copy(f32[256,256]{1,0:T(8,128)S(1)} %get-tuple-element.4) | data formatting | bytes 524288
  38.5 0.7 %copy.7 = f32[256,256]{1,0:T(8,128)} copy(f32[256,256]{1,0:T(8,128)S(1)} %get-tuple-element.5) | data formatting | bytes 524288
Async XLA Ops:
  0.6 1.0 %copy-start = (f32[256,256]{1,0:T(8,128)S(1)}, f32[256,256]{1,0:T(8,128)}, u32[]{:S(2)}) copy-start(f32[256,256]{1,0:T(8,128)} %pos_ref.1) | copy-start | bytes 786436
  1.6 0.9 %copy-start.1 = (f32[256,256]{1,0:T(8,128)S(1)}, f32[256,256]{1,0:T(8,128)}, u32[]{:S(2)}) copy-start(f32[256,256]{1,0:T(8,128)} %neg_ref.1) | copy-start | bytes 786436

commit v2 on v1

v2 whole, which is shorter than its diff:
```python
import functools

import jax
import jax.numpy as jnp
from jax import lax
from jax.experimental import pallas as pl
from jax.experimental.pallas import tpu as pltpu
from jax.sharding import PartitionSpec as P

STEPS = 2
NEWTON = 4
PIECE = 16
GROUPS = 4
MESH = pl.DeviceIdType.MESH


def split(a):
    high = a.astype(jnp.bfloat16)
    low = (a - high.astype(jnp.float32)).astype(jnp.bfloat16)
    return high, low


def mm(a, b):
    dot = functools.partial(jnp.dot, preferred_element_type=jnp.float32)
    return dot(a[0], b[0]) + (dot(a[0], b[1]) + dot(a[1], b[0]))


def eye_mask(size):
    rows = lax.broadcasted_iota(jnp.int32, (size, size), 0)
    cols = lax.broadcasted_iota(jnp.int32, (size, size), 1)
    return rows == cols


def solve(lead_p, lead_n):
    mask = eye_mask(lead_p.shape[0])
    diagonal = jnp.where(mask, lead_p, 0.0)
    inv_rows = 1.0 / jnp.sum(diagonal, axis=1, keepdims=True)
    inv_cols = 1.0 / jnp.sum(diagonal, axis=0, keepdims=True)
    power = jnp.where(mask, 1.0, 0.0) - inv_rows * lead_p
    acc = lead_n
    for index in range(NEWTON):
        power_s = split(power)
        acc = acc + mm(split(acc), power_s)
        if index < NEWTON - 1:
            power = mm(power_s, power_s)
    return acc * inv_cols


def root_less_one(gram):
    mask = eye_mask(gram.shape[0])
    gram_s = split(gram)
    square = mm(gram_s, gram_s)
    inner = jnp.where(mask, 0.375, 0.0) + 0.3125 * gram + 0.2734375 * square
    return 0.5 * gram + mm(split(square), split(inner))


def roots_from(kt):
    c_s = split(kt.T)
    k_s = split(kt)
    s_top = root_less_one(mm(c_s, k_s))
    s_bottom = root_less_one(mm(k_s, c_s))
    return c_s, k_s, split(s_top), split(s_bottom)


def reflect(c_s, s_s, main, other):
    wide = main - mm(c_s, split(other))
    return wide + mm(s_s, split(wide))


def kernel(n, pos_hbm, neg_hbm, pos_out, neg_out, pos_ref, neg_ref, lead, nb, kbuf, pair, own1,
           in_sem, sc_send, ag_send, bc_recv, core_send, core_recv,
           nb_send, nb_recv, rel_send, ld_send, ld_recv):
    me = lax.axis_index("blk")
    size = pos_ref.shape[0]
    chips = n // 2
    holders = min(chips, size // PIECE)
    rows = size // holders
    per_group = holders // GROUPS
    group_rows = size // GROUPS
    chip = me // 2
    even = me % 2 == 0
    has_next = me + 1 < n
    to_second = even & (me + 2 < n)
    holds = even & (chip < holders)

    loads = [pltpu.make_async_copy(src, dst, in_sem.at[i])
             for i, (src, dst) in enumerate(((pos_hbm, pos_ref), (neg_hbm, neg_ref)))]
    for load in loads:
        load.start()

    barrier = pltpu.get_barrier_semaphore()

    def greet(device):
        pl.semaphore_signal(barrier, inc=1, device_id=(device,), device_id_type=MESH)

    @pl.when(me >= 1)
    def _():
        greet(me - 1)

    @pl.when(has_next)
    def _():
        greet(me + 1)

    @pl.when(even)
    def _():
        def greet_chip(t, carry):
            greet(2 * lax.rem(chip + t, chips))
            return carry

        lax.fori_loop(1, chips, greet_chip, 0)

    count = (jnp.where(me >= 1, 1, 0) + jnp.where(has_next, 1, 0)
             + jnp.where(even, chips - 1, 0))

    @pl.when(me == 0)
    def _():
        for load in loads:
            load.wait()
        kbuf[0] = solve(pos_ref[...], neg_ref[...])
        nb[...] = jnp.zeros_like(nb)

    pl.semaphore_wait(barrier, count)

    def remote(src, dst, send, recv, device):
        return pltpu.make_async_remote_copy(
            src_ref=src, dst_ref=dst, send_sem=send, recv_sem=recv,
            device_id=(device,), device_id_type=MESH)

    hbm = (pos_hbm, neg_hbm)
    next_copies = [remote(hbm[i], nb.at[i], nb_send.at[i], nb_recv.at[i], me + 1) for i in range(2)]
    second_copies = [remote(hbm[i], nb.at[2 + i], nb_send.at[2 + i], nb_recv.at[2 + i], me + 2)
                     for i in range(2)]
    relay_copies = [remote(nb.at[i], nb.at[2 + i], rel_send.at[i], nb_recv.at[2 + i], me + 1)
                    for i in range(2)]
    lead_copies = [remote(hbm[i], lead.at[i], ld_send.at[i], ld_recv.at[i], 0) for i in range(2)]

    def start(copies):
        for copy in copies:
            copy.start()

    def piece_of(step, piece):
        return kbuf.at[step, pl.ds(pl.multiple_of(piece * rows, rows), rows)]

    def scatter_copy(step, piece):
        part = piece_of(step, piece)
        return remote(part, part, sc_send.at[step, piece], bc_recv.at[step, piece], 2 * piece)

    def gather_copy(step, target):
        part = piece_of(step, chip)
        return remote(part, part, ag_send.at[step, target], bc_recv.at[step, chip], 2 * target)

    def core_copy(step, group):
        part = kbuf.at[step, pl.ds(group * group_rows, group_rows)]
        return remote(part, part, core_send.at[step, group], core_recv.at[step, group], me + 1)

    def each_target(step, act):
        def one(t, carry):
            target = lax.rem(chip + t, chips)

            @pl.when(target != 0)
            def _():
                act(gather_copy(step, target))

            return carry

        lax.fori_loop(1, chips, one, 0)

    def each_scatter(step, act):
        def one(t, carry):
            act(scatter_copy(step, t))
            return carry

        lax.fori_loop(1, holders, one, 0)

    def publish(step):
        each_scatter(step, lambda copy: copy.start())
        each_target(step, lambda copy: copy.start())
        for group in range(GROUPS):
            core_copy(step, group).start()

    def receive(step):
        @pl.when(holds)
        def _():
            scatter_copy(step, chip).wait_recv()
            each_target(step, lambda copy: copy.start())

        @pl.when(even)
        def _():
            for group in range(GROUPS):
                for piece in range(group * per_group, (group + 1) * per_group):
                    @pl.when(chip != piece)
                    def _(piece=piece):
                        scatter_copy(step, piece).wait_recv()

                core_copy(step, group).start()

        @pl.when(jnp.logical_not(even))
        def _():
            for group in range(GROUPS):
                core_copy(step, group).wait_recv()

    @pl.when(me == 0)
    def _():
        publish(0)

    @pl.when(me == 1)
    def _():
        start(lead_copies)

    @pl.when(has_next)
    def _():
        start(next_copies)

    @pl.when(to_second)
    def _():
        start(second_copies)

    @pl.when(me >= 1)
    def _():
        for load in loads:
            load.wait()
        receive(0)
        for copy in next_copies:
            copy.wait_recv()

    @pl.when(even & (me >= 2))
    def _():
        start(relay_copies)

    @pl.when(me == 1)
    def _():
        nb[2] = jnp.zeros((size, size), jnp.float32)
        nb[3] = jnp.zeros((size, size), jnp.float32)

    for i, pair_part in enumerate(roots_from(kbuf[0])):
        pair[i, 0] = pair_part[0]
        pair[i, 1] = pair_part[1]

    def loaded():
        return [(pair[i, 0], pair[i, 1]) for i in range(4)]

    @pl.when(me == 0)
    def _():
        c1, k1, st1, sb1 = loaded()
        for copy in lead_copies:
            copy.wait_recv()
        lead_p = reflect(c1, st1, pos_ref[...], neg_ref[...])
        lead_n = reflect(k1, sb1, lead[1], lead[0])
        kbuf[1] = solve(lead_p, lead_n)
        publish(1)

    @pl.when(me >= 2)
    def _():
        for copy in second_copies:
            copy.wait_recv()

    c1, k1, st1, sb1 = loaded()
    own1[0] = reflect(k1, sb1, neg_ref[...], pos_ref[...])
    own1[1] = reflect(c1, st1, nb[0], nb[1])
    own1[2] = reflect(k1, sb1, nb[1], nb[0])
    own1[3] = reflect(c1, st1, nb[2], nb[3])

    @pl.when(me >= 1)
    def _():
        receive(1)

    c2, k2, st2, sb2 = roots_from(kbuf[1])
    neg_out[...] = reflect(k2, sb2, own1[0], own1[1])
    pos_out[...] = reflect(c2, st2, own1[3], own1[2])

    def sent(copies):
        for copy in copies:
            copy.wait_send()

    @pl.when(has_next)
    def _():
        sent(next_copies)

    @pl.when(me == 1)
    def _():
        sent(lead_copies)

    @pl.when(to_second)
    def _():
        sent(second_copies)

    @pl.when(even & (me >= 2))
    def _():
        sent(relay_copies)

    for step in range(STEPS):
        @pl.when(me == 0)
        def _(step=step):
            each_scatter(step, lambda copy: copy.wait_send())

        @pl.when(holds)
        def _(step=step):
            each_target(step, lambda copy: copy.wait_send())

        @pl.when(even)
        def _(step=step):
            for group in range(GROUPS):
                core_copy(step, group).wait_send()


def solution(mesh):
    n = mesh.shape["blk"]

    def on_device(positive_row, negative_row):
        size = positive_row.shape[0]
        block = jax.ShapeDtypeStruct((size, size), jnp.float32)
        chips = n // 2
        holders = min(chips, size // PIECE)
        dma = pltpu.SemaphoreType.DMA
        vmem = pl.BlockSpec(memory_space=pltpu.VMEM)
        hbm = pl.BlockSpec(memory_space=pltpu.HBM)
        return pl.pallas_call(
            functools.partial(kernel, n),
            out_shape=(block, block),
            in_specs=[hbm, hbm],
            out_specs=(vmem, vmem),
            scratch_shapes=[
                pltpu.VMEM((size, size), jnp.float32),
                pltpu.VMEM((size, size), jnp.float32),
                pltpu.VMEM((2, size, size), jnp.float32),
                pltpu.VMEM((4, size, size), jnp.float32),
                pltpu.VMEM((STEPS, size, size), jnp.float32),
                pltpu.VMEM((4, 2, size, size), jnp.bfloat16),
                pltpu.VMEM((4, size, size), jnp.float32),
                dma((2,)), dma((STEPS, holders)), dma((STEPS, chips)), dma((STEPS, holders)),
                dma((STEPS, GROUPS)), dma((STEPS, GROUPS)),
                dma((4,)), dma((4,)), dma((2,)), dma((2,)), dma((2,)),
            ],
            compiler_params=pltpu.CompilerParams(
                collective_id=0, has_side_effects=True, vmem_limit_bytes=64 * 2**20),
        )(positive_row, negative_row)

    spec = (P(None, "blk"), P(None, "blk"))
    return jax.shard_map(on_device, mesh=mesh, in_specs=spec, out_specs=spec, check_vma=False)
```

time: 39.4 us -> 39.1 us (level)
  the two profiles are of different devices: /device:TPU:31 before, /device:TPU:5 now
where the time goes in v2:
time: 39.1 us; the launch traced here: 39 us
  Pallas kernels  35.9 us (92%)
  local copies, waits for them, and re-layouts  2.42 us (6%)
  between operations  0.65 us (2%)
    pallas_call x1, Pallas kernels, on_device(): pl.pallas_call(functools.partial(kernel, n), out_shape=(block, block), in...  35.9 us
    unnamed x4, local copies, waits for them, and re-layouts  2.42 us

profile of v2, /device:TPU:5, one launch (start us, length us, event | category | flops | bytes accessed | tf_op | source)
XLA Modules:
  0.0 39.0 jit_solution(13700702612695463792)
XLA Ops:
  0.6 35.9 %shard_map.41 = (f32[256,256]{1,0:T(8,128)}, f32[256,256]{1,0:T(8,128)}) custom-call(f32[256,256]{1,0:T(8,128)} %pos_hbm.1, f32[256,256]{1,0:T(8,128)} %neg_hbm.1), custom_call_target="tpu_custom_call" | custom-call | tf_op jit(solution)/shard_map/pallas_call | solution.py:317
  36.5 0.0 copy-start
  36.5 1.7 %copy.6 = f32[256,256]{1,0:T(8,128)} copy(f32[256,256]{1,0:T(8,128)} %get-tuple-element.4) | data formatting | bytes 524288
  38.3 0.0 copy-done
  38.3 0.7 %copy.7 = f32[256,256]{1,0:T(8,128)} copy(f32[256,256]{1,0:T(8,128)S(1)} %copy-done) | data formatting | bytes 524288
Async XLA Ops:
  36.5 1.7 %copy-start = (f32[256,256]{1,0:T(8,128)S(1)}, f32[256,256]{1,0:T(8,128)}, u32[]{:S(2)}) copy-start(f32[256,256]{1,0:T(8,128)} %get-tuple-element.5) | copy-start | bytes 786436

commit v3 on v2

--- a/solution.py
+++ b/solution.py
@@ -69,7 +69,7 @@
 
 def kernel(n, pos_hbm, neg_hbm, pos_out, neg_out, pos_ref, neg_ref, lead, nb, kbuf, pair, own1,
            in_sem, sc_send, ag_send, bc_recv, core_send, core_recv,
-           nb_send, nb_recv, rel_send, ld_send, ld_recv):
+           nb_send, nb_recv, sh_send, sh_recv, ld_send, ld_recv):
     me = lax.axis_index("blk")
     size = pos_ref.shape[0]
     chips = n // 2
@@ -80,7 +80,6 @@
     chip = me // 2
     even = me % 2 == 0
     has_next = me + 1 < n
-    to_second = even & (me + 2 < n)
     holds = even & (chip < holders)
 
     loads = [pltpu.make_async_copy(src, dst, in_sem.at[i])
@@ -128,10 +127,7 @@
 
     hbm = (pos_hbm, neg_hbm)
     next_copies = [remote(hbm[i], nb.at[i], nb_send.at[i], nb_recv.at[i], me + 1) for i in range(2)]
-    second_copies = [remote(hbm[i], nb.at[2 + i], nb_send.at[2 + i], nb_recv.at[2 + i], me + 2)
-                     for i in range(2)]
-    relay_copies = [remote(nb.at[i], nb.at[2 + i], rel_send.at[i], nb_recv.at[2 + i], me + 1)
-                    for i in range(2)]
+    shift_copy = remote(own1.at[1], own1.at[3], sh_send, sh_recv, me + 1)
     lead_copies = [remote(hbm[i], lead.at[i], ld_send.at[i], ld_recv.at[i], 0) for i in range(2)]
 
     def start(copies):
@@ -211,10 +207,6 @@
     def _():
         start(next_copies)
 
-    @pl.when(to_second)
-    def _():
-        start(second_copies)
-
     @pl.when(me >= 1)
     def _():
         for load in loads:
@@ -222,15 +214,6 @@
         receive(0)
         for copy in next_copies:
             copy.wait_recv()
-
-    @pl.when(even & (me >= 2))
-    def _():
-        start(relay_copies)
-
-    @pl.when(me == 1)
-    def _():
-        nb[2] = jnp.zeros((size, size), jnp.float32)
-        nb[3] = jnp.zeros((size, size), jnp.float32)
 
     for i, pair_part in enumerate(roots_from(kbuf[0])):
         pair[i, 0] = pair_part[0]
@@ -249,20 +232,24 @@
         kbuf[1] = solve(lead_p, lead_n)
         publish(1)
 
-    @pl.when(me >= 2)
-    def _():
-        for copy in second_copies:
-            copy.wait_recv()
-
     c1, k1, st1, sb1 = loaded()
+    own1[1] = reflect(c1, st1, nb[0], nb[1])
+
+    @pl.when(has_next)
+    def _():
+        shift_copy.start()
+
     own1[0] = reflect(k1, sb1, neg_ref[...], pos_ref[...])
-    own1[1] = reflect(c1, st1, nb[0], nb[1])
     own1[2] = reflect(k1, sb1, nb[1], nb[0])
-    own1[3] = reflect(c1, st1, nb[2], nb[3])
 
     @pl.when(me >= 1)
     def _():
         receive(1)
+        shift_copy.wait_recv()
+
+    @pl.when(me == 0)
+    def _():
+        own1[3] = jnp.zeros((size, size), jnp.float32)
 
     c2, k2, st2, sb2 = roots_from(kbuf[1])
     neg_out[...] = reflect(k2, sb2, own1[0], own1[1])
@@ -274,19 +261,11 @@
 
     @pl.when(has_next)
     def _():
-        sent(next_copies)
+        sent(next_copies + [shift_copy])
 
     @pl.when(me == 1)
     def _():
         sent(lead_copies)
-
-    @pl.when(to_second)
-    def _():
-        sent(second_copies)
-
-    @pl.when(even & (me >= 2))
-    def _():
-        sent(relay_copies)
 
     for step in range(STEPS):
         @pl.when(me == 0)
@@ -308,7 +287,6 @@
 
     def on_device(positive_row, negative_row):
         size = positive_row.shape[0]
-        block = jax.ShapeDtypeStruct((size, size), jnp.float32)
         chips = n // 2
         holders = min(chips, size // PIECE)
         dma = pltpu.SemaphoreType.DMA
@@ -316,23 +294,23 @@
         hbm = pl.BlockSpec(memory_space=pltpu.HBM)
         return pl.pallas_call(
             functools.partial(kernel, n),
-            out_shape=(block, block),
+            out_shape=(pltpu.VMEM((size, size), jnp.float32),) * 2,
             in_specs=[hbm, hbm],
             out_specs=(vmem, vmem),
             scratch_shapes=[
                 pltpu.VMEM((size, size), jnp.float32),
                 pltpu.VMEM((size, size), jnp.float32),
                 pltpu.VMEM((2, size, size), jnp.float32),
-                pltpu.VMEM((4, size, size), jnp.float32),
+                pltpu.VMEM((2, size, size), jnp.float32),
                 pltpu.VMEM((STEPS, size, size), jnp.float32),
                 pltpu.VMEM((4, 2, size, size), jnp.bfloat16),
                 pltpu.VMEM((4, size, size), jnp.float32),
                 dma((2,)), dma((STEPS, holders)), dma((STEPS, chips)), dma((STEPS, holders)),
                 dma((STEPS, GROUPS)), dma((STEPS, GROUPS)),
-                dma((4,)), dma((4,)), dma((2,)), dma((2,)), dma((2,)),
+                dma((2,)), dma((2,)), dma, dma, dma((2,)), dma((2,)),
             ],
             compiler_params=pltpu.CompilerParams(
-                collective_id=0, has_side_effects=True, vmem_limit_bytes=64 * 2**20),
+                collective_id=0, has_side_effects=True, vmem_limit_bytes=64000000),
         )(positive_row, negative_row)
 
     spec = (P(None, "blk"), P(None, "blk"))

time: 39.1 us -> 32.6 us (0.83)
  the two profiles are of different devices: /device:TPU:5 before, /device:TPU:16 now
where the time goes in v3:
time: 32.6 us; the launch traced here: 32.5 us
  Pallas kernels  30.4 us (93%)
  local copies, waits for them, and re-layouts  1.41 us (4%)
  between operations  0.64 us (2%)
    pallas_call x1, Pallas kernels, on_device(): pl.pallas_call(functools.partial(kernel, n), out_shape=(pltpu.VMEM((size,...  30.4 us
    unnamed x2, local copies, waits for them, and re-layouts  1.41 us

profile of v3, /device:TPU:16, one launch (start us, length us, event | category | flops | bytes accessed | tf_op | source)
XLA Modules:
  0.0 32.5 jit_solution(13098240584688525774)
XLA Ops:
  0.6 30.4 %shard_map.41 = (f32[256,256]{1,0:T(8,128)S(1)}, f32[256,256]{1,0:T(8,128)S(1)}) custom-call(f32[256,256]{1,0:T(8,128)} %pos_hbm.1, f32[256,256]{1,0:T(8,128)} %neg_hbm.1), custom_call_target="tpu_custom_call" | custom-call | tf_op jit(solution)/shard_map/pallas_call | solution.py:295
  31.1 0.7 %copy.6 = f32[256,256]{1,0:T(8,128)} copy(f32[256,256]{1,0:T(8,128)S(1)} %get-tuple-element.2) | data formatting | bytes 524288
  31.8 0.7 %copy.7 = f32[256,256]{1,0:T(8,128)} copy(f32[256,256]{1,0:T(8,128)S(1)} %get-tuple-element.3) | data formatting | bytes 524288

commit v4 on v3

--- a/solution.py
+++ b/solution.py
@@ -80,7 +80,8 @@
     chip = me // 2
     even = me % 2 == 0
     has_next = me + 1 < n
-    holds = even & (chip < holders)
+    relays = even & (me > 0)
+    holds = (relays & (chip < holders)) | (me == 1)
 
     loads = [pltpu.make_async_copy(src, dst, in_sem.at[i])
              for i, (src, dst) in enumerate(((pos_hbm, pos_ref), (neg_hbm, neg_ref)))]
@@ -108,8 +109,21 @@
 
         lax.fori_loop(1, chips, greet_chip, 0)
 
+    @pl.when(me == 1)
+    def _():
+        def greet_even(t, carry):
+            greet(2 * t)
+            return carry
+
+        lax.fori_loop(2, chips, greet_even, 0)
+
+    @pl.when(even & (chip >= 2))
+    def _():
+        greet(1)
+
     count = (jnp.where(me >= 1, 1, 0) + jnp.where(has_next, 1, 0)
-             + jnp.where(even, chips - 1, 0))
+             + jnp.where(even, chips - 1, 0) + jnp.where(me == 1, chips - 2, 0)
+             + jnp.where(even & (chip >= 2), 1, 0))
 
     @pl.when(me == 0)
     def _():
@@ -169,13 +183,13 @@
         lax.fori_loop(1, holders, one, 0)
 
     def publish(step):
+        core_copy(step, 0).start()
         each_scatter(step, lambda copy: copy.start())
-        each_target(step, lambda copy: copy.start())
-        for group in range(GROUPS):
+        for group in range(1, GROUPS):
             core_copy(step, group).start()
 
     def receive(step):
-        @pl.when(holds)
+        @pl.when(holds & even)
         def _():
             scatter_copy(step, chip).wait_recv()
             each_target(step, lambda copy: copy.start())
@@ -194,6 +208,10 @@
         def _():
             for group in range(GROUPS):
                 core_copy(step, group).wait_recv()
+                if group == 0:
+                    @pl.when(me == 1)
+                    def _():
+                        each_target(step, lambda copy: copy.start())
 
     @pl.when(me == 0)
     def _():

time: 32.6 us -> 34.4 us (1.055)
  Pallas kernels: 30.4 us -> 32.2 us
    pallas_call x1, Pallas kernels: 30.4 us -> 32.2 us  [on_device(): pl.pallas_call(functools.partial(kernel, n), out_shape=(pltpu.VMEM((size,...]
where the time goes in v4:
time: 34.4 us; the launch traced here: 34.3 us
  Pallas kernels  32.2 us (94%)
  local copies, waits for them, and re-layouts  1.41 us (4%)
  between operations  0.64 us (2%)
    pallas_call x1, Pallas kernels, on_device(): pl.pallas_call(functools.partial(kernel, n), out_shape=(pltpu.VMEM((size,...  32.2 us
    unnamed x2, local copies, waits for them, and re-layouts  1.41 us

profile of v4, /device:TPU:16, one launch (start us, length us, event | category | flops | bytes accessed | tf_op | source)
XLA Modules:
  0.0 34.3 jit_solution(7497142707330246531)
XLA Ops:
  0.6 32.2 %shard_map.41 = (f32[256,256]{1,0:T(8,128)S(1)}, f32[256,256]{1,0:T(8,128)S(1)}) custom-call(f32[256,256]{1,0:T(8,128)} %pos_hbm.1, f32[256,256]{1,0:T(8,128)} %neg_hbm.1), custom_call_target="tpu_custom_call" | custom-call | tf_op jit(solution)/shard_map/pallas_call | solution.py:313
  32.9 0.7 %copy.6 = f32[256,256]{1,0:T(8,128)} copy(f32[256,256]{1,0:T(8,128)S(1)} %get-tuple-element.2) | data formatting | bytes 524288
  33.6 0.7 %copy.7 = f32[256,256]{1,0:T(8,128)} copy(f32[256,256]{1,0:T(8,128)S(1)} %get-tuple-element.3) | data formatting | bytes 524288

commit v5 on v3

--- a/solution.py
+++ b/solution.py
@@ -12,6 +12,18 @@
 PIECE = 16
 GROUPS = 4
 MESH = pl.DeviceIdType.MESH
+
+
+def repeat(first, last, body):
+    if last - first <= 32:
+        for t in range(first, last):
+            body(t)
+    else:
+        def one(t, carry):
+            body(t)
+            return carry
+
+        lax.fori_loop(first, last, one, 0)
 
 
 def split(a):
@@ -138,39 +150,38 @@
         return kbuf.at[step, pl.ds(pl.multiple_of(piece * rows, rows), rows)]
 
     def scatter_copy(step, piece):
-        part = piece_of(step, piece)
+        part = kbuf.at[step, pl.ds(piece * rows if isinstance(piece, int)
+                                   else pl.multiple_of(piece * rows, rows), rows)]
         return remote(part, part, sc_send.at[step, piece], bc_recv.at[step, piece], 2 * piece)
 
     def gather_copy(step, target):
         part = piece_of(step, chip)
         return remote(part, part, ag_send.at[step, target], bc_recv.at[step, chip], 2 * target)
 
+    def root_copy(step, target):
+        part = kbuf.at[step, pl.ds(0, rows)]
+        return remote(part, part, ag_send.at[step, target], bc_recv.at[step, 0], 2 * target)
+
     def core_copy(step, group):
         part = kbuf.at[step, pl.ds(group * group_rows, group_rows)]
         return remote(part, part, core_send.at[step, group], core_recv.at[step, group], me + 1)
 
     def each_target(step, act):
-        def one(t, carry):
+        def one(t):
             target = lax.rem(chip + t, chips)
 
             @pl.when(target != 0)
             def _():
                 act(gather_copy(step, target))
 
-            return carry
-
-        lax.fori_loop(1, chips, one, 0)
+        repeat(1, chips, one)
 
     def each_scatter(step, act):
-        def one(t, carry):
-            act(scatter_copy(step, t))
-            return carry
-
-        lax.fori_loop(1, holders, one, 0)
+        repeat(1, holders, lambda t: act(scatter_copy(step, t)))
 
     def publish(step):
         each_scatter(step, lambda copy: copy.start())
-        each_target(step, lambda copy: copy.start())
+        repeat(1, chips, lambda t: root_copy(step, t).start())
         for group in range(GROUPS):
             core_copy(step, group).start()
 

time: 32.6 us -> 32.5 us (level)
  no operation moved by 1% of the time
where the time goes in v5:
time: 32.5 us; the launch traced here: 32.4 us
  Pallas kernels  30.3 us (93%)
  local copies, waits for them, and re-layouts  1.41 us (4%)
  between operations  0.64 us (2%)
    pallas_call x1, Pallas kernels, on_device(): pl.pallas_call(functools.partial(kernel, n), out_shape=(pltpu.VMEM((size,...  30.3 us
    unnamed x2, local copies, waits for them, and re-layouts  1.41 us

profile of v5, /device:TPU:16, one launch (start us, length us, event | category | flops | bytes accessed | tf_op | source)
XLA Modules:
  0.0 32.4 jit_solution(15682498633779527721)
XLA Ops:
  0.6 30.3 %shard_map.41 = (f32[256,256]{1,0:T(8,128)S(1)}, f32[256,256]{1,0:T(8,128)S(1)}) custom-call(f32[256,256]{1,0:T(8,128)} %pos_hbm.1, f32[256,256]{1,0:T(8,128)} %neg_hbm.1), custom_call_target="tpu_custom_call" | custom-call | tf_op jit(solution)/shard_map/pallas_call | solution.py:306
  31.0 0.7 %copy.6 = f32[256,256]{1,0:T(8,128)} copy(f32[256,256]{1,0:T(8,128)S(1)} %get-tuple-element.2) | data formatting | bytes 524288
  31.7 0.7 %copy.7 = f32[256,256]{1,0:T(8,128)} copy(f32[256,256]{1,0:T(8,128)S(1)} %get-tuple-element.3) | data formatting | bytes 524288
